TPU v7x, 256 devices: a whole 4x4x8 slice. The times are simulated.
256 devices in a mesh: dp: 16 (over z_hi, x), ctx: 16 (over z_lo, y, core).
Axes of the slice: x: 4, y: 4, z: 8 (z_hi: 4, z_lo: 2; z = z_hi * 2 + z_lo), core: 2. Of those that a mesh axis runs over, the one named last changes fastest.
Arguments:
- queries: bfloat16 [16, 2, 16, 64, 2048], P('dp', None, 'ctx'), may hold values from -24 to 24
- key_states: bfloat16 [16, 2, 16, 64, 512], P('dp', None, 'ctx'), may hold values from -24 to 24
- value_vectors: bfloat16 [16, 2, 16, 64, 512], P('dp', None, 'ctx'), may hold values from -6 to 6
- grad_out: bfloat16 [16, 2, 16, 64, 2048], P('dp', None, 'ctx'), may hold values from -6 to 6
- doc_start: int32 [16, 2, 16, 64], P('dp', None, 'ctx'), may hold values from 0 to 32767, as said below
Outputs:
- attn_out: bfloat16 [16, 2, 16, 64, 2048], P('dp', None, 'ctx')
- q_grad: bfloat16 [16, 2, 16, 64, 2048], P('dp', None, 'ctx')
- k_grad: bfloat16 [16, 2, 16, 64, 512], P('dp', None, 'ctx')
- v_grad: bfloat16 [16, 2, 16, 64, 512], P('dp', None, 'ctx')
Inputs may be any that keep to these rules, and one draw needn't show every extreme that they name: Every token from doc_start of a token to that token's own position belongs to its document and carries the same doc_start; documents have at most 2048 tokens and one has exactly 2048; every document except the sequence's last token, which is a document of its own, has at least 512 tokens; a document that reaches into the positions of cycle d from an earlier cycle begins at or after position d * 2048 - 2048 // 2.
All inputs are finite; a program needn't handle non-finite values.
Results may differ from a plain program's by a relative error of at most 0.027.
Values may be sent and summed in bfloat16 or wider, within the bound.
No kernel may reach another device: no remote copies, remote signals or barrier semaphores. Data moves between devices by JAX's collectives and lax.ppermute only.
A program may use at most 128 MiB of HBM per device.

v0:
```python
import math

import jax
import jax.numpy as jnp
from jax import lax
from jax.sharding import PartitionSpec as P

HEAD_SIZE = 128


NEG_FILL = -1e30


def passed_along(block, axis, distance):
    devices = range(lax.axis_size(axis))
    route = [(i - distance, i) for i in devices if i - distance in devices]
    return lax.ppermute(block, axis, route)


def on_device(queries, key_states, value_vectors, grad_out, doc_start):
    half_rows = queries.shape[3]
    local_rows = 2 * half_rows
    width_q = queries.shape[4]
    width_kv = key_states.shape[4]
    kv_heads = width_kv // HEAD_SIZE
    query_group_size = width_q // width_kv
    members = lax.axis_size("ctx")
    cycle_id = lax.axis_index("dp")
    member_id = lax.axis_index("ctx")
    cycle_span = local_rows * members
    score_scale = HEAD_SIZE ** (-0.5)
    query_rows = queries.reshape(local_rows, kv_heads, query_group_size, HEAD_SIZE)
    grad_rows = grad_out.reshape(local_rows, kv_heads, query_group_size, HEAD_SIZE)
    states = jnp.stack(
        [key_states.reshape(local_rows, width_kv), value_vectors.reshape(local_rows, width_kv)],
        axis=1,
    )
    offsets = jnp.arange(half_rows, dtype=jnp.int32)
    query_pos = cycle_id * cycle_span + jnp.concatenate(
        [member_id * half_rows + offsets, (2 * members - 1 - member_id) * half_rows + offsets]
    )
    query_start = doc_start.reshape(local_rows)
    tail_rows = passed_along(states[half_rows:], "dp", 1)
    own_states, prev_states = (
        lax.all_gather(states, "ctx", axis=0, tiled=True),
        lax.all_gather(tail_rows, "ctx", axis=0, tiled=True),
    )
    own_index = jnp.arange(cycle_span, dtype=jnp.int32)
    owner = own_index // local_rows
    upper = own_index % local_rows // half_rows
    own_block = jnp.where(upper == 0, owner, 2 * members - 1 - owner)
    own_pos = cycle_id * cycle_span + own_block * half_rows + own_index % half_rows
    prev_index = jnp.arange(cycle_span // 2, dtype=jnp.int32)
    prev_pos = (
        (cycle_id - 1) * cycle_span
        + (2 * members - 1 - prev_index // half_rows) * half_rows
        + prev_index % half_rows
    )
    all_states = jnp.concatenate([own_states, prev_states], axis=0)
    all_pos = jnp.concatenate([own_pos, prev_pos])
    keys_total = all_states.shape[0]
    block_rows = math.gcd(keys_total, 512)
    block_count = keys_total // block_rows
    key_blocks = all_states.reshape(block_count, block_rows, 2, width_kv)
    pos_blocks = all_pos.reshape(block_count, block_rows)

    def visible_of(key_pos):
        return (key_pos[None, :] >= query_start[:, None]) & (key_pos[None, :] <= query_pos[:, None])

    def scores_of(state_block):
        key_block = state_block[:, 0].reshape(block_rows, kv_heads, HEAD_SIZE)
        return (
            jnp.einsum("qgjd,kgd->gjqk", query_rows, key_block, preferred_element_type=jnp.float32)
            * score_scale
        )

    def stats_step(carry, item):
        state_block, key_pos = item
        visible_pairs = visible_of(key_pos)
        max_old, total_old = carry
        scores = jnp.where(visible_pairs, scores_of(state_block), NEG_FILL)
        max_new = jnp.maximum(max_old, jnp.max(scores, axis=-1))
        total_new = total_old * jnp.exp(max_old - max_new) + jnp.sum(
            jnp.exp(scores - max_new[..., None]), axis=-1
        )
        return ((max_new, total_new), None)

    start_max = jnp.full((kv_heads, query_group_size, local_rows), NEG_FILL, jnp.float32)
    start_total = jnp.zeros((kv_heads, query_group_size, local_rows), jnp.float32)
    (row_max, row_total), _ = lax.scan(
        stats_step, (start_max, start_total), (key_blocks, pos_blocks)
    )
    lse = row_max + jnp.log(row_total)

    def probs_of(state_block, visible_pairs):
        return jnp.where(visible_pairs, jnp.exp(scores_of(state_block) - lse[..., None]), 0.0)

    def out_step(carry, item):
        state_block, key_pos = item
        visible_pairs = visible_of(key_pos)
        probs = probs_of(state_block, visible_pairs).astype(jnp.bfloat16)
        value_block = state_block[:, 1].reshape(block_rows, kv_heads, HEAD_SIZE)
        return (
            carry
            + jnp.einsum("gjqk,kgd->qgjd", probs, value_block, preferred_element_type=jnp.float32),
            None,
        )

    zero_rows = jnp.zeros((local_rows, kv_heads, query_group_size, HEAD_SIZE), jnp.float32)
    out_sum, _ = lax.scan(out_step, zero_rows, (key_blocks, pos_blocks))
    attn = out_sum.astype(jnp.bfloat16)
    delta = jnp.sum(attn.astype(jnp.float32) * grad_rows.astype(jnp.float32), axis=-1).transpose(
        1, 2, 0
    )

    def grad_step(carry, item):
        state_block, key_pos = item
        visible_pairs = visible_of(key_pos)
        key_block = state_block[:, 0].reshape(block_rows, kv_heads, HEAD_SIZE)
        value_block = state_block[:, 1].reshape(block_rows, kv_heads, HEAD_SIZE)
        probs_full = probs_of(state_block, visible_pairs)
        probs = probs_full.astype(jnp.bfloat16)
        dprobs = jnp.einsum(
            "qgjd,kgd->gjqk", grad_rows, value_block, preferred_element_type=jnp.float32
        )
        dscores = (probs_full * (dprobs - delta[..., None])).astype(jnp.bfloat16)
        q_next = carry + jnp.einsum(
            "gjqk,kgd->qgjd", dscores, key_block, preferred_element_type=jnp.float32
        )
        k_part = (
            jnp.einsum("gjqk,qgjd->kgd", dscores, query_rows, preferred_element_type=jnp.float32)
            * score_scale
        )
        v_part = jnp.einsum("gjqk,qgjd->kgd", probs, grad_rows, preferred_element_type=jnp.float32)
        return (
            q_next,
            jnp.stack(
                [k_part.reshape(block_rows, width_kv), v_part.reshape(block_rows, width_kv)], axis=1
            ),
        )

    q_sum, key_terms = lax.scan(grad_step, zero_rows, (key_blocks, pos_blocks))
    q_grad = (q_sum * score_scale).astype(jnp.bfloat16)
    key_terms = key_terms.reshape(keys_total, 2, width_kv)
    own_terms = key_terms[:cycle_span]
    prev_terms = key_terms[cycle_span:]
    own_part, prev_part = (
        lax.psum_scatter(own_terms, "ctx", scatter_dimension=0, tiled=True),
        lax.psum_scatter(prev_terms, "ctx", scatter_dimension=0, tiled=True),
    )
    returned = passed_along(prev_part.astype(jnp.bfloat16), "dp", -1).astype(prev_part.dtype)
    total = own_part + jnp.concatenate([jnp.zeros_like(returned), returned], axis=0)
    k_grad = total[:, 0].astype(jnp.bfloat16).reshape(key_states.shape)
    v_grad = total[:, 1].astype(jnp.bfloat16).reshape(value_vectors.shape)
    return (attn.reshape(queries.shape), q_grad.reshape(queries.shape), k_grad, v_grad)


def solution(mesh):
    in_specs = (
        P("dp", None, "ctx", None, None),
        P("dp", None, "ctx", None, None),
        P("dp", None, "ctx", None, None),
        P("dp", None, "ctx", None, None),
        P("dp", None, "ctx", None),
    )
    out_specs = (
        P("dp", None, "ctx", None, None),
        P("dp", None, "ctx", None, None),
        P("dp", None, "ctx", None, None),
        P("dp", None, "ctx", None, None),
    )
    return jax.shard_map(
        on_device, mesh=mesh, in_specs=in_specs, out_specs=out_specs, check_vma=False
    )
```

profile of v0, /device:TPU:70, one launch (start us, length us, event | category | flops | bytes accessed | tf_op | source)
XLA Modules:
  0.0 408.5 jit_solution(16197992492584731469)
XLA Ops:
  8.2 6.3 %collective-permute-start = (bf16[64,2,512]{2,0,1:T(8,128)(2,1)S(1)}, bf16[64,2,512]{2,0,1:T(8,128)(2,1)S(1)}, u32[]{:S(2)}, u32[]{:S(2)}) collective-permute-start(bf16[64,2,512]{2,0,1:T(8,128)(2,1)S(1)} %fusion.25), channel_id=1, source_target_pairs={{0,16},{16,32},{32,48},{48,64},{64,80},{80,96},{96,112},{112,128},... | collective-permute-start | bytes 393224 | tf_op jit(solution)/shard_map/ppermute | solution.py:17
  14.5 5.4 %collective-permute-done = bf16[64,2,512]{2,0,1:T(8,128)(2,1)S(1)} collective-permute-done((bf16[64,2,512]{2,0,1:T(8,128)(2,1)S(1)}, bf16[64,2,512]{2,0,1:T(8,128)(2,1)S(1)}, u32[]{:S(2)}, u32[]{:S(2)}) %collective-permute-start) | collective-permute-done | bytes 131104 | tf_op jit(solution)/shard_map/ppermute | solution.py:17
  20.6 1.7 pad_maximum_fusion.1
  24.7 1.4 reshape.71
  28.5 30.8 %all-gather.5.cloned.1.call-done = bf16[1024,2,512]{2,0,1:T(8,128)(2,1)} async-done(((bf16[64,2,512]{2,0,1:T(8,128)(2,1)}), bf16[1024,2,512]{2,0,1:T(8,128)(2,1)}) %all-gather.5.cloned.1.call-update) | async-done | bytes 2097168 | tf_op jit(solution)/shard_map/all_gather | solution.py:46
  59.3 42.2 %all-gather.3.cloned.1.call-done = bf16[2048,2,512]{2,0,1:T(8,128)(2,1)} async-done(((bf16[128,2,512]{2,0,1:T(8,128)(2,1)}), bf16[2048,2,512]{2,0,1:T(8,128)(2,1)}) %all-gather.3.cloned.1.call-update) | async-done | bytes 4194320 | tf_op jit(solution)/shard_map/all_gather | solution.py:45
  101.6 5.8 %pad_maximum_fusion = bf16[3072,2,512]{2,0,1:T(8,128)(2,1)} fusion(bf16[1024,2,512]{2,0,1:T(8,128)(2,1)} %all-gather.5.cloned.1.call-done, bf16[2048,2,512]{2,0,1:T(8,128)(2,1)} %all-gather.3.cloned.1.call-done), kind=kLoop, calls=%fused_computation.44 | loop fusion | flops 12582912 | bytes 12582912 | tf_op jit(solution)/shard_map/concatenate | solution.py:59
  107.4 8.7 %copy.114 = bf16[6,512,2,512]{1,3,2,0:T(8,128)(2,1)} copy(bf16[6,512,2,512]{3,1,0,2:T(8,128)(2,1)} %bitcast.258) | data formatting | bytes 12582912
  116.1 19.9 %while.40 = (s32[]{:T(128)}, f32[4,4,128]{2,1,0:T(4,128)S(1)}, f32[4,4,128]{2,1,0:T(4,128)S(1)}, s32[6,512]{1,0:T(8,128)S(1)}, s32[1,2,1,64]{3,1,2,0:T(2,128)}, ...) while((s32[]{:T(128)}, f32[4,4,128]{2,1,0:T(4,128)S(1)}, ...), condition=%wide.wide.region_3.4_spmd.clone, body=%wide.wide.region_0.3_spmd.clone.sunk | while | flops 275982336 | bytes 12893320 | solution.py:90
  126.2 1.3 dynamic-slice_bitcast_fusion.9
  129.5 1.3 dynamic-slice_bitcast_fusion.9
  136.0 29.1 %while.41 = (s32[]{:T(128)}, f32[128,4,4,128]{0,3,2,1:T(8,128)}, bf16[6,512,2,512]{1,3,2,0:T(8,128)(2,1)}, s32[6,512]{1,0:T(8,128)S(1)}, s32[1,2,1,64]{3,1,2,0:T...) while((s32[]{:T(128)}, f32[128,4,4,128]{0,3,2,1:T(8,128)}, ...), condition=%wide.wide.region_5.6_spmd.clone, body=%wide.wide.region_4.5_spmd.clone.sunk | while | flops 541786112 | bytes 8010887 | solution.py:110
  136.2 1.3 dynamic-slice_bitcast_fusion.10
  137.5 2.3 fusion.132
  141.4 3.5 fusion.132
  146.4 3.5 fusion.132
  151.5 3.5 fusion.132
  155.2 1.3 dynamic-slice_bitcast_fusion.10
  156.5 3.5 fusion.132
  160.2 1.3 dynamic-slice_bitcast_fusion.10
  161.6 3.5 fusion.132
  165.1 1.7 copy.117
  167.7 80.6 %while.42 = (s32[]{:T(128)}, f32[128,4,4,128]{0,3,2,1:T(8,128)}, f32[6,512,2,512]{3,1,0,2:T(8,128)}, bf16[6,512,2,512]{1,3,2,0:T(8,128)(2,1)}, s32[6,512]{1,0:T(...) while((s32[]{:T(128)}, f32[128,4,4,128]{0,3,2,1:T(8,128)}, ...), condition=%wide.wide.region_8.9_spmd.clone, body=%wide.wide.region_7.8_spmd.clone.sunk | while | flops 1354170368 | bytes 45841596 | solution.py:142
  167.9 1.3 dynamic-slice_bitcast_fusion.11
  171.2 1.5 fusion.145
  172.8 1.6 fusion.146
  175.2 1.5 maximum_bitcast_fusion.3
  176.7 1.9 copy.156
  178.7 1.5 constant_dynamic-update-slice_fusion.3
  180.3 1.3 dynamic-slice_bitcast_fusion.11
  183.7 1.5 fusion.145
  185.2 2.8 fusion.146
  188.8 1.5 maximum_bitcast_fusion.3
  190.4 1.9 copy.156
  192.3 1.6 constant_dynamic-update-slice_fusion.3
  197.3 1.5 fusion.145
  198.9 2.8 fusion.146
  202.5 1.5 maximum_bitcast_fusion.3
  204.0 1.9 copy.156
  206.0 1.6 constant_dynamic-update-slice_fusion.3
  207.7 1.3 dynamic-slice_bitcast_fusion.11
  211.0 1.5 fusion.145
  212.5 2.8 fusion.146
  216.2 1.5 maximum_bitcast_fusion.3
  217.7 1.9 copy.156
  219.6 1.5 constant_dynamic-update-slice_fusion.3
  224.6 1.5 fusion.145
  226.1 2.8 fusion.146
  229.8 1.5 maximum_bitcast_fusion.3
  231.3 1.9 copy.156
  233.2 1.5 constant_dynamic-update-slice_fusion.3
  234.9 1.3 dynamic-slice_bitcast_fusion.11
  238.2 1.5 fusion.145
  239.7 2.8 fusion.146
  243.4 1.5 maximum_bitcast_fusion.3
  244.9 1.9 copy.156
  246.8 1.5 constant_dynamic-update-slice_fusion.3
  248.3 4.6 %slice.42 = f32[2,512,2,512]{3,1,0,2:T(8,128)} slice(f32[6,512,2,512]{3,1,0,2:T(8,128)} %get-tuple-element.151), slice={[4:6], [0:512], [0:2], [0:512]} | slice | bytes 8388608 | tf_op jit(solution)/shard_map/slice | solution.py:146
  253.0 7.6 %slice.40 = f32[4,512,2,512]{3,1,0,2:T(8,128)} slice(f32[6,512,2,512]{3,1,0,2:T(8,128)} %get-tuple-element.151), slice={[0:4], [0:512], [0:2], [0:512]} | slice | bytes 16777216 | tf_op jit(solution)/shard_map/slice | solution.py:145
  260.6 62.0 %reduce-scatter.5.cloned.1.call-done = f32[64,2,512]{2,0,1:T(8,128)} async-done(((f32[1024,2,512]{2,0,1:T(8,128)}), f32[64,2,512]{2,0,1:T(8,128)}) %reduce-scatter.5.cloned.1.call-update) | async-done | bytes 262160 | tf_op jit(solution)/shard_map/reduce_scatter | solution.py:149
  323.5 2.8 collective-permute-start.1
  326.3 1.4 multiply_convert_fusion
  330.5 5.5 %collective-permute-done.1 = bf16[64,2,512]{2,0,1:T(8,128)(2,1)S(1)} collective-permute-done((bf16[64,2,512]{2,0,1:T(8,128)(2,1)S(1)}, bf16[64,2,512]{2,0,1:T(8,128)(2,1)S(1)}, u32[]{:S(2)}, u32[]{:S(2)}) %collective-permute-start.1) | collective-permute-done | bytes 131104 | tf_op jit(solution)/shard_map/ppermute | solution.py:17
  335.9 64.2 %reduce-scatter.3.cloned.1.call-done = f32[128,2,512]{2,0,1:T(8,128)} async-done(((f32[2048,2,512]{2,0,1:T(8,128)}), f32[128,2,512]{2,0,1:T(8,128)}) %reduce-scatter.3.cloned.1.call-update) | async-done | bytes 524304 | tf_op jit(solution)/shard_map/reduce_scatter | solution.py:148
  (163 shorter events, 55.3 us)
Async XLA Ops:
  7.2 19.7 %copy-start = (bf16[1,2,1,64,2048]{4,3,2,1,0:T(8,128)(2,1)S(1)}, bf16[1,2,1,64,2048]{4,3,2,1,0:T(8,128)(2,1)}, u32[]{:S(2)}) copy-start(bf16[1,2,1,64,2048]{4,3,2,1,0:T(8,128)(2,1)} %param.14) | copy-start | bytes 1572868
  7.2 52.1 %all-gather.5.cloned.1.call-start = ((), (), s32[]{:S(2)}) async-start(), calls=%async_computation.3 | async-start | bytes 2228224 | tf_op jit(solution)/shard_map/all_gather | solution.py:46
  8.2 11.8 %collective-permute-start = (bf16[64,2,512]{2,0,1:T(8,128)(2,1)S(1)}, bf16[64,2,512]{2,0,1:T(8,128)(2,1)S(1)}, u32[]{:S(2)}, u32[]{:S(2)}) collective-permute-start(bf16[64,2,512]{2,0,1:T(8,128)(2,1)S(1)} %fusion.25), channel_id=1, source_target_pairs={{0,16},{16,32},{32,48},{48,64},{64,80},{80,96},{96,112},{112,128},... | collective-permute-start | bytes 393224 | tf_op jit(solution)/shard_map/ppermute | solution.py:17
  19.9 0.7 copy-start.2
  20.6 81.0 %all-gather.3.cloned.1.call-start = ((), (), s32[]{:S(2)}) async-start(), calls=%async_computation.2 | async-start | bytes 4456448 | tf_op jit(solution)/shard_map/all_gather | solution.py:45
  22.4 300.2 %reduce-scatter.5.cloned.1.call-start = ((), (), s32[]{:S(2)}) async-start(), calls=%async_computation.5 | async-start | bytes 4456448 | tf_op jit(solution)/shard_map/reduce_scatter | solution.py:149
  169.2 1.0 copy-start.1
  181.6 1.0 copy-start.1
  195.3 1.0 copy-start.1
  209.0 1.0 copy-start.1
  222.6 1.0 copy-start.1
  236.2 1.0 copy-start.1
  253.0 147.2 %reduce-scatter.3.cloned.1.call-start = ((), (), s32[]{:S(2)}) async-start(), calls=%async_computation.4 | async-start | bytes 8912896 | tf_op jit(solution)/shard_map/reduce_scatter | solution.py:148
  323.5 12.4 %collective-permute-start.1 = (bf16[64,2,512]{2,0,1:T(8,128)(2,1)S(1)}, bf16[64,2,512]{2,0,1:T(8,128)(2,1)S(1)}, u32[]{:S(2)}, u32[]{:S(2)}) collective-permute-start(bf16[64,2,512]{2,0,1:T(8,128)(2,1)S(1)} %convert_element_type.51), channel_id=1, source_target_pairs={{16,0},{32,16},{48,32},{64,48},{80,64},{96,80},{112,96},{128,112},... | collective-permute-start | bytes 393224 | tf_op jit(solution)/shard_map/ppermute | solution.py:17
Sparse Core Ops, SparseCore 0:
  20.7 38.5 all-gather.4
  61.7 39.8 all-gather.2
  253.1 69.4 reduce-scatter.4
  325.0 75.1 reduce-scatter.2
where the time goes:
time: 412 us; the launch traced here: 409 us
  waiting for transfers between devices  210 us (51%)
  local copies, waits for them, and re-layouts  79.1 us (19%)
  matrix products  65.1 us (16%)
  other arithmetic  30 us (7%)
  between operations  13.9 us (3%)
  starting transfers between devices  9.25 us (2%)
    reduce_scatter x1, waiting for transfers between devices, on_device(): lax.psum_scatter(own_terms, 'ctx', scatter_dimension=0, tiled=True)  64.2 us
    reduce_scatter x1, waiting for transfers between devices, on_device(): lax.psum_scatter(prev_terms, 'ctx', scatter_dimension=0, tiled=True)  62 us
    all_gather x1, waiting for transfers between devices, on_device(): lax.all_gather(states, 'ctx', axis=0, tiled=True)  42.2 us
    all_gather x1, waiting for transfers between devices, on_device(): lax.all_gather(tail_rows, 'ctx', axis=0, tiled=True)  30.8 us
    squeeze x18, local copies, waits for them, and re-layouts, on_device(): lax.scan(stats_step, (start_max, start_total), (key_blocks, pos_blocks))  23.4 us
    dynamic_update_slice x12, local copies, waits for them, and re-layouts, on_device(): q_sum, key_terms = lax.scan(grad_step, zero_rows, (key_blocks, pos_blocks))  20.7 us
    dot_general x6, matrix products, out_step(): jnp.einsum('gjqk,kgd->qgjd', probs, value_block, preferred_element_type=j...  19.9 us
    dot_general x6, matrix products, grad_step(): jnp.einsum('gjqk,kgd->qgjd', dscores, key_block, preferred_element_type=j...  15.7 us
  transfers between devices with their start and end apart: 6, of which 6 were waited for; matrix products, arithmetic and copies ran while one was open for 5% of the time, Pallas kernels for 0%

commit v1 on v0

v1 whole, which is shorter than its diff:
```python
import jax
import jax.numpy as jnp
from jax import lax
from jax.experimental import pallas as pl
from jax.experimental.pallas import tpu as pltpu
from jax.sharding import PartitionSpec as P

HEAD = 128
HALF = 64
MEMBERS = 16
HEADS = 16
GROUPS = 4
SPAN = 2048
BACK = 1024
KEYS = SPAN + BACK
TQ = 256
TK = 512
SCALE = HEAD**-0.5
LOG2E = 1.4426950408889634
NEG = -1e30

RQ, RG, RK, RV, RPK, RPV, RS = 0, 128, 256, 384, 512, 576, 640
ROWS_IN = 656
ROWS_OUT = 640

NT = (((1,), (1,)), ((), ()))
NN = (((1,), (0,)), ((), ()))


def dot(a, b, dims=NN):
    return lax.dot_general(a, b, dims, preferred_element_type=jnp.float32)


def pack_kernel(q_ref, g_ref, k_ref, v_ref, tail_ref, s_ref, o_ref):
    for n in range(HEADS):
        g = n // (HEADS // GROUPS)
        at = slice(n * HEAD, (n + 1) * HEAD)
        kv = slice(g * HEAD, (g + 1) * HEAD)
        o_ref[n, RQ : RQ + 128] = q_ref[:, at]
        o_ref[n, RG : RG + 128] = g_ref[:, at]
        o_ref[n, RK : RK + 128] = k_ref[:, kv]
        o_ref[n, RV : RV + 128] = v_ref[:, kv]
        o_ref[n, RPK : RPK + 64] = tail_ref[0:64, kv]
        o_ref[n, RPV : RPV + 64] = tail_ref[64:128, kv]
        o_ref[n, RS : RS + 16] = s_ref[...]


def attn_kernel(r_ref, o_ref, q_s, g_s, k_s, v_s, kt_s, vt_s, st_s, p_s, dq_s, dk_s, dv_s):
    for s in range(MEMBERS):
        lo, hi = 64 * s, 64 * (31 - s)
        q_s[lo : lo + 64] = r_ref[s, RQ : RQ + 64]
        q_s[hi : hi + 64] = r_ref[s, RQ + 64 : RQ + 128]
        g_s[lo : lo + 64] = r_ref[s, RG : RG + 64]
        g_s[hi : hi + 64] = r_ref[s, RG + 64 : RG + 128]
        k_s[BACK + lo : BACK + lo + 64] = r_ref[s, RK : RK + 64]
        k_s[BACK + hi : BACK + hi + 64] = r_ref[s, RK + 64 : RK + 128]
        v_s[BACK + lo : BACK + lo + 64] = r_ref[s, RV : RV + 64]
        v_s[BACK + hi : BACK + hi + 64] = r_ref[s, RV + 64 : RV + 128]
        pv = 64 * (15 - s)
        k_s[pv : pv + 64] = r_ref[s, RPK : RPK + 64]
        v_s[pv : pv + 64] = r_ref[s, RPV : RPV + 64]
    for t in range(SPAN // 128):
        s0, s1, row = (2 * t, 2 * t + 1, 0) if t < 8 else (31 - 2 * t, 30 - 2 * t, 2)
        both = r_ref[s0, RS : RS + 16].astype(jnp.float32) + r_ref[s1, RS : RS + 16].astype(
            jnp.float32
        )
        start = both[row : row + 1] * 64.0 + both[row + 1 : row + 2]
        st_s[t // 2, 0:1, (t % 2) * 128 : (t % 2) * 128 + 128] = start.astype(jnp.int32)
    for t in range(KEYS // 256):
        at = slice(256 * t, 256 * t + 256)
        kt_s[:, at] = k_s[at].T
        vt_s[:, at] = v_s[at].T
    dk_s[...] = jnp.zeros_like(dk_s)
    dv_s[...] = jnp.zeros_like(dv_s)

    lanes = lax.broadcasted_iota(jnp.int32, (1, TQ), 1)
    rows = lax.broadcasted_iota(jnp.int32, (TK, TQ), 0)
    fold = SCALE * LOG2E

    def q_block(i, _):
        q_at = pl.ds(pl.multiple_of(i * TQ, TQ), TQ)
        qi = q_s[q_at, :]
        gi = g_s[q_at, :]
        start = st_s[i, 0:1, :]
        last = BACK + i * TQ + lanes
        first_tile = jnp.min(start) // TK
        end_tile = (BACK + i * TQ + TQ - 1) // TK + 1

        def stats(t, m8):
            at = pl.ds(pl.multiple_of(t * TK, TK), TK)
            s = dot(k_s[at, :], qi, NT)
            seen = (rows >= start - t * TK) & (rows <= last - t * TK)
            s = jnp.where(seen, s, NEG)
            p_s[at, :] = s
            return jnp.maximum(m8, jnp.max(s.reshape(TK // 8, 8, TQ), axis=0))

        m8 = lax.fori_loop(first_tile, end_tile, stats, jnp.full((8, TQ), NEG, jnp.float32))
        m = jnp.max(m8, axis=0, keepdims=True) * fold

        def outs(t, carry):
            l8, acc = carry
            at = pl.ds(pl.multiple_of(t * TK, TK), TK)
            p = jnp.exp2(p_s[at, :] * fold - m)
            p_s[at, :] = p
            l8 = l8 + jnp.sum(p.reshape(TK // 8, 8, TQ), axis=0)
            acc = acc + dot(vt_s[:, at], p.astype(jnp.bfloat16))
            return l8, acc

        l8, acc = lax.fori_loop(
            first_tile,
            end_tile,
            outs,
            (jnp.zeros((8, TQ), jnp.float32), jnp.zeros((HEAD, TQ), jnp.float32)),
        )
        inv = 1.0 / jnp.sum(l8, axis=0, keepdims=True)
        out_t = acc * inv
        delta = jnp.sum(out_t * gi.astype(jnp.float32).T, axis=0, keepdims=True)
        q_s[q_at, :] = out_t.T.astype(jnp.bfloat16)

        def grads(t, dq):
            at = pl.ds(pl.multiple_of(t * TK, TK), TK)
            p = p_s[at, :] * inv
            dp = dot(v_s[at, :], gi, NT)
            ds = (p * (dp - delta)).astype(jnp.bfloat16)
            dv_s[at, :] += dot(p.astype(jnp.bfloat16), gi)
            dk_s[at, :] += dot(ds, qi)
            return dq + dot(kt_s[:, at], ds)

        dq = lax.fori_loop(first_tile, end_tile, grads, jnp.zeros((HEAD, TQ), jnp.float32))
        dq_s[q_at, :] = (dq * SCALE).T.astype(jnp.bfloat16)
        return 0

    lax.fori_loop(0, SPAN // TQ, q_block, 0)

    for s in range(MEMBERS):
        lo, hi = 64 * s, 64 * (31 - s)
        o_ref[s, RQ : RQ + 64] = q_s[lo : lo + 64]
        o_ref[s, RQ + 64 : RQ + 128] = q_s[hi : hi + 64]
        o_ref[s, RG : RG + 64] = dq_s[lo : lo + 64]
        o_ref[s, RG + 64 : RG + 128] = dq_s[hi : hi + 64]
        for row, src, c in ((RK, dk_s, SCALE), (RV, dv_s, 1.0)):
            o_ref[s, row : row + 64] = (src[BACK + lo : BACK + lo + 64] * c).astype(jnp.bfloat16)
            o_ref[s, row + 64 : row + 128] = (src[BACK + hi : BACK + hi + 64] * c).astype(
                jnp.bfloat16
            )
        pv = 64 * (15 - s)
        o_ref[s, RPK : RPK + 64] = (dk_s[pv : pv + 64] * SCALE).astype(jnp.bfloat16)
        o_ref[s, RPV : RPV + 64] = dv_s[pv : pv + 64].astype(jnp.bfloat16)


def back_kernel(t_ref, o_ref):
    for g in range(GROUPS):
        total = t_ref[4 * g].astype(jnp.float32)
        for j in range(1, 4):
            total = total + t_ref[4 * g + j].astype(jnp.float32)
        o_ref[:, g * HEAD : (g + 1) * HEAD] = total.astype(jnp.bfloat16)


def unpack_kernel(t_ref, b_ref, a_ref, q_ref, k_ref, v_ref):
    for n in range(HEADS):
        at = slice(n * HEAD, (n + 1) * HEAD)
        a_ref[:, at] = t_ref[n, RQ : RQ + 128]
        q_ref[:, at] = t_ref[n, RG : RG + 128]
    for g in range(GROUPS):
        at = slice(g * HEAD, (g + 1) * HEAD)
        for row, back, o_ref in ((RK, 0, k_ref), (RV, 64, v_ref)):
            total = t_ref[4 * g, row : row + 128].astype(jnp.float32)
            for j in range(1, 4):
                total = total + t_ref[4 * g + j, row : row + 128].astype(jnp.float32)
            o_ref[0:64, at] = total[0:64].astype(jnp.bfloat16)
            o_ref[64:128, at] = (
                total[64:128] + b_ref[back : back + 64, at].astype(jnp.float32)
            ).astype(jnp.bfloat16)


def params(mib):
    return pltpu.CompilerParams(vmem_limit_bytes=mib * 1024 * 1024)


def on_device(queries, key_states, value_vectors, grad_out, doc_start):
    cycle = lax.axis_index("dp")
    member = lax.axis_index("ctx")
    bf = jnp.bfloat16
    q = queries.reshape(128, HEADS * HEAD)
    g = grad_out.reshape(128, HEADS * HEAD)
    k = key_states.reshape(128, GROUPS * HEAD)
    v = value_vectors.reshape(128, GROUPS * HEAD)

    tail = jnp.concatenate([k[64:], v[64:]], axis=0)
    tail = lax.ppermute(tail, "dp", [(i, i + 1) for i in range(15)])

    rel = doc_start.reshape(2, 1, HALF) - (cycle * SPAN - BACK)
    parts = jnp.concatenate([rel // 64, rel % 64], axis=1).astype(bf)
    zero = jnp.zeros_like(parts)
    first = jnp.concatenate([parts, zero], axis=2)
    second = jnp.concatenate([zero, parts], axis=2)
    even = member % 2 == 0
    starts = jnp.concatenate(
        [jnp.where(even, first[0], second[0]), jnp.where(even, second[1], first[1])], axis=0
    )
    starts = jnp.concatenate([starts, jnp.zeros((12, 128), bf)], axis=0)

    sent = pl.pallas_call(
        pack_kernel,
        out_shape=jax.ShapeDtypeStruct((HEADS, ROWS_IN, HEAD), bf),
        compiler_params=params(24),
        name="pack",
    )(q, g, k, v, tail, starts)
    got = lax.all_to_all(sent, "ctx", 0, 0, tiled=True)
    sums = pl.pallas_call(
        attn_kernel,
        out_shape=jax.ShapeDtypeStruct((MEMBERS, ROWS_OUT, HEAD), bf),
        scratch_shapes=[
            pltpu.VMEM((SPAN, HEAD), bf),
            pltpu.VMEM((SPAN, HEAD), bf),
            pltpu.VMEM((KEYS, HEAD), bf),
            pltpu.VMEM((KEYS, HEAD), bf),
            pltpu.VMEM((HEAD, KEYS), bf),
            pltpu.VMEM((HEAD, KEYS), bf),
            pltpu.VMEM((SPAN // TQ, 8, TQ), jnp.int32),
            pltpu.VMEM((KEYS, TQ), jnp.float32),
            pltpu.VMEM((SPAN, HEAD), bf),
            pltpu.VMEM((KEYS, HEAD), jnp.float32),
            pltpu.VMEM((KEYS, HEAD), jnp.float32),
        ],
        compiler_params=params(48),
        name="attention",
    )(got)
    home = lax.all_to_all(sums, "ctx", 0, 0, tiled=True)
    back = pl.pallas_call(
        back_kernel,
        out_shape=jax.ShapeDtypeStruct((128, GROUPS * HEAD), bf),
        compiler_params=params(24),
        name="back",
    )(home[:, RPK:])
    back = lax.ppermute(back, "dp", [(i + 1, i) for i in range(15)])
    attn, q_grad, k_grad, v_grad = pl.pallas_call(
        unpack_kernel,
        out_shape=[
            jax.ShapeDtypeStruct(q.shape, bf),
            jax.ShapeDtypeStruct(q.shape, bf),
            jax.ShapeDtypeStruct(k.shape, bf),
            jax.ShapeDtypeStruct(k.shape, bf),
        ],
        compiler_params=params(24),
        name="unpack",
    )(home, back)
    return (
        attn.reshape(queries.shape),
        q_grad.reshape(queries.shape),
        k_grad.reshape(key_states.shape),
        v_grad.reshape(value_vectors.shape),
    )


def solution(mesh):
    wide = P("dp", None, "ctx", None, None)
    return jax.shard_map(
        on_device,
        mesh=mesh,
        in_specs=(wide, wide, wide, wide, P("dp", None, "ctx", None)),
        out_specs=(wide, wide, wide, wide),
        check_vma=False,
    )
```

time: 412 us -> 132 us (0.32)
  waiting for transfers between devices: 210 us -> 19 us
  blocking collectives: 0 us -> 74.4 us
  local copies, waits for them, and re-layouts: 79.1 us -> 4.89 us
  matrix products: 65.1 us -> 0 us
  other arithmetic: 30 us -> 0.88 us
  Pallas kernels: 0 us -> 22.3 us
  between operations: 13.9 us -> 0.72 us
    reduce_scatter x2 -> x0, waiting for transfers between devices: 126 us -> none  [the longest x1 64.2 us: on_device(): lax.psum_scatter(own_terms, 'ctx', scatter_dimension=0, tiled=True)]
    all_to_all x0 -> x2, blocking collectives: none -> 74.4 us  [the longest x1 38.4 us: on_device(): got = lax.all_to_all(sent, 'ctx', 0, 0, tiled=True)]
    all_gather x2 -> x0, waiting for transfers between devices: 73 us -> none  [the longest x1 42.2 us: on_device(): lax.all_gather(states, 'ctx', axis=0, tiled=True)]
    dot_general x42 -> x0, matrix products: 65.1 us -> none  [the longest x6 19.9 us: out_step(): jnp.einsum('gjqk,kgd->qgjd', probs, value_block, preferred_element_type=j...]
    squeeze x18 -> x0, local copies, waits for them, and re-layouts: 23.4 us -> none  [on_device(): lax.scan(stats_step, (start_max, start_total), (key_blocks, pos_blocks))]
    pallas_call x0 -> x4, Pallas kernels: none -> 22.3 us  [the longest x1 20.5 us: on_device(): pl.pallas_call(attn_kernel, out_shape=jax.ShapeDtypeStruct((MEMBERS, ROWS...]
    dynamic_update_slice x12 -> x0, local copies, waits for them, and re-layouts: 20.7 us -> none  [on_device(): q_sum, key_terms = lax.scan(grad_step, zero_rows, (key_blocks, pos_blocks))]
    slice x21 -> x2, local copies, waits for them, and re-layouts: 13.9 us -> 0.93 us  [the longest x1 0.89 us: on_device(): tail = jnp.concatenate([k[64:], v[64:]], axis=0)]
  transfers between devices with their start and end apart: 6 -> 2, of which waited for: 6 -> 2; matrix products, arithmetic and copies ran while one was open for 5% -> 1% of each run, Pallas kernels for 0% -> 0%
where the time goes in v1:
time: 132 us; the launch traced here: 130 us
  blocking collectives  74.4 us (56%)
  Pallas kernels  22.3 us (17%)
  waiting for transfers between devices  19 us (14%)
  starting transfers between devices  8.23 us (6%)
  local copies, waits for them, and re-layouts  4.89 us (4%)
    all_to_all x1, blocking collectives, on_device(): got = lax.all_to_all(sent, 'ctx', 0, 0, tiled=True)  38.4 us
    all_to_all x1, blocking collectives, on_device(): home = lax.all_to_all(sums, 'ctx', 0, 0, tiled=True)  36 us
    pallas_call x1, Pallas kernels, on_device(): pl.pallas_call(attn_kernel, out_shape=jax.ShapeDtypeStruct((MEMBERS, ROWS...  20.5 us
    ppermute x1, waiting for transfers between devices, on_device(): back = lax.ppermute(back, 'dp', [(i + 1, i) for i in range(15)])  14.5 us
    ppermute x1, starting transfers between devices, on_device(): tail = lax.ppermute(tail, 'dp', [(i, i + 1) for i in range(15)])  6.3 us
    ppermute x1, waiting for transfers between devices, on_device(): tail = lax.ppermute(tail, 'dp', [(i, i + 1) for i in range(15)])  4.47 us
    unnamed x8, local copies, waits for them, and re-layouts  3.89 us
  transfers between devices with their start and end apart: 2, of which 2 were waited for; matrix products, arithmetic and copies ran while one was open for 1% of the time, Pallas kernels for 0%

profile of v1, /device:TPU:70, one launch (start us, length us, event | category | flops | bytes accessed | tf_op | source)
XLA Modules:
  0.0 130.4 jit_solution(18402983931998893745)
XLA Ops:
  0.6 0.9 slice_bitcast_fusion
  1.5 6.3 %collective-permute-start = (bf16[128,512]{1,0:T(8,128)(2,1)S(1)}, bf16[128,512]{1,0:T(8,128)(2,1)S(1)}, u32[]{:S(2)}, u32[]{:S(2)}) collective-permute-start(bf16[128,512]{1,0:T(8,128)(2,1)S(1)} %pad_maximum_fusion), channel_id=1, source_target_pairs={{0,16},{16,32},{32,48},{48,64},{64,80},{80,96},{96,112},{112,128},... | collective-permute-start | bytes 393224 | tf_op jit(solution)/shard_map/ppermute | solution.py:190
  7.9 0.7 fusion.1
  8.6 0.1 pad.4.clone
  8.7 0.1 fusion.2
  8.7 0.1 maximum_maximum_fusion.s_ref
  8.8 4.5 %collective-permute-done.tail_ref = bf16[128,512]{1,0:T(8,128)(2,1)S(1)} collective-permute-done((bf16[128,512]{1,0:T(8,128)(2,1)S(1)}, bf16[128,512]{1,0:T(8,128)(2,1)S(1)}, u32[]{:S(2)}, u32[]{:S(2)}) %collective-permute-start) | collective-permute-done | bytes 131104 | tf_op jit(solution)/shard_map/ppermute | solution.py:190
  13.3 0.0 copy-start
  13.3 1.0 copy-done
  14.3 0.0 copy-start.1
  14.3 1.0 copy-done.1
  15.4 0.0 copy-start.2
  15.4 0.9 copy-done.2
  16.3 0.0 copy-start.3
  16.3 0.9 copy-done.3
  17.2 0.4 pack.1
  17.6 38.4 %all_to_all.10.r_ref = bf16[16,656,128]{2,1,0:T(8,128)(2,1)S(1)} all-to-all(bf16[16,656,128]{2,1,0:T(8,128)(2,1)S(1)} %pack.1), channel_id=1, replica_groups=mesh['dp'=16,'ctx'=16] {'ctx'}, dimensions={0} | all-to-all | bytes 5373952 | tf_op jit(solution)/shard_map/all_to_all | solution.py:209
  56.0 20.5 %attention.1 = bf16[16,640,128]{2,1,0:T(8,128)(2,1)S(1)} custom-call(bf16[16,656,128]{2,1,0:T(8,128)(2,1)S(1)} %all_to_all.10.r_ref), custom_call_target="tpu_custom_call" | custom-call | tf_op jit(solution)/shard_map/attention/pallas_call | solution.py:210
  76.5 36.0 %all_to_all.11.t_ref = bf16[16,640,128]{2,1,0:T(8,128)(2,1)S(1)} all-to-all(bf16[16,640,128]{2,1,0:T(8,128)(2,1)S(1)} %attention.1), channel_id=1, replica_groups=mesh['dp'=16,'ctx'=16] {'ctx'}, dimensions={0} | all-to-all | bytes 5242880 | tf_op jit(solution)/shard_map/all_to_all | solution.py:229
  112.5 0.1 back.1
  112.6 1.9 %collective-permute-start.1 = (bf16[128,512]{1,0:T(8,128)(2,1)S(1)}, bf16[128,512]{1,0:T(8,128)(2,1)S(1)}, u32[]{:S(2)}, u32[]{:S(2)}) collective-permute-start(bf16[128,512]{1,0:T(8,128)(2,1)S(1)} %back.1), channel_id=1, source_target_pairs={{16,0},{32,16},{48,32},{64,48},{80,64},{96,80},{112,96},{128,112},... | collective-permute-start | bytes 393224 | tf_op jit(solution)/shard_map/ppermute | solution.py:236
  114.5 14.5 %collective-permute-done.1.b_ref = bf16[128,512]{1,0:T(8,128)(2,1)S(1)} collective-permute-done((bf16[128,512]{1,0:T(8,128)(2,1)S(1)}, bf16[128,512]{1,0:T(8,128)(2,1)S(1)}, u32[]{:S(2)}, u32[]{:S(2)}) %collective-permute-start.1) | collective-permute-done | bytes 131104 | tf_op jit(solution)/shard_map/ppermute | solution.py:236
  129.1 1.4 %unpack.1 = (bf16[128,2048]{1,0:T(8,128)(2,1)}, bf16[128,2048]{1,0:T(8,128)(2,1)}, bf16[128,512]{1,0:T(8,128)(2,1)}, bf16[128,512]{1,0:T(8,128)(2,1)}) custom-call(bf16[16,640,128]{2,1,0:T(8,128)(2,1)S(1)} %all_to_all.11.t_ref, bf16[128,512]{1,0:T(8,128)(2,1)S(1)} %collective-permute-done.1.b_ref), custom_call_target="tpu_custom_call" | custom-call | tf_op jit(solution)/shard_map/unpack/pallas_call | solution.py:237
  (5 shorter events, 0.1 us)
Async XLA Ops:
  1.5 11.8 %collective-permute-start = (bf16[128,512]{1,0:T(8,128)(2,1)S(1)}, bf16[128,512]{1,0:T(8,128)(2,1)S(1)}, u32[]{:S(2)}, u32[]{:S(2)}) collective-permute-start(bf16[128,512]{1,0:T(8,128)(2,1)S(1)} %pad_maximum_fusion), channel_id=1, source_target_pairs={{0,16},{16,32},{32,48},{48,64},{64,80},{80,96},{96,112},{112,128},... | collective-permute-start | bytes 393224 | tf_op jit(solution)/shard_map/ppermute | solution.py:190
  13.3 1.0 copy-start
  14.3 1.0 copy-start.1
  15.4 0.9 copy-start.2
  16.3 0.9 copy-start.3
  112.6 16.4 %collective-permute-start.1 = (bf16[128,512]{1,0:T(8,128)(2,1)S(1)}, bf16[128,512]{1,0:T(8,128)(2,1)S(1)}, u32[]{:S(2)}, u32[]{:S(2)}) collective-permute-start(bf16[128,512]{1,0:T(8,128)(2,1)S(1)} %back.1), channel_id=1, source_target_pairs={{16,0},{32,16},{48,32},{64,48},{80,64},{96,80},{112,96},{128,112},... | collective-permute-start | bytes 393224 | tf_op jit(solution)/shard_map/ppermute | solution.py:236

commit v2 on v1

v2 whole, which is shorter than its diff:
```python
import jax
import jax.numpy as jnp
from jax import lax
from jax.experimental import pallas as pl
from jax.experimental.pallas import tpu as pltpu
from jax.sharding import PartitionSpec as P

HEAD = 128
HALF = 64
MEMBERS = 16
HEADS = 16
GROUPS = 4
SPAN = 2048
BACK = 1024
TQ = 512
TK = 256
QB = SPAN // TQ
QS = TQ // HALF
KS = TK // HALF
OWN_TILES = SPAN // TK
BACK_TILES = BACK // TK
SCALE = HEAD**-0.5
FOLD = SCALE * 1.4426950408889634
NEG = -1e30
BF = jnp.bfloat16
F32 = jnp.float32

IN_Q, IN_G, IN_X, IN_S, IN_ROWS = 0, 128, 256, 384, 400
OUT_A, OUT_Q, OUT_X, OUT_ROWS = 0, 128, 256, 384

NT = (((1,), (1,)), ((), ()))
NN = (((1,), (0,)), ((), ()))


def dot(a, b, dims=NN):
    return lax.dot_general(a, b, dims, preferred_element_type=F32)


def begin(pairs, sems):
    copies = [pltpu.make_async_copy(a, b, sems.at[i]) for i, (a, b) in enumerate(pairs)]
    for c in copies:
        c.start()
    return copies


def finish(copies):
    for c in copies:
        c.wait()


def columns(n):
    return pl.ds(n * HEAD, HEAD)


def halves(ref, row, to, at=0):
    return [
        (ref.at[:, pl.ds(row, HALF)], to.at[pl.ds(at, MEMBERS)]),
        (ref.at[:, pl.ds(row + HALF, HALF)], to.at[pl.ds(at + MEMBERS, MEMBERS)]),
    ]


def pack_kernel(q_ref, g_ref, k_ref, v_ref, s_ref, o_ref, sems):
    pairs = []
    for n in range(HEADS):
        x_ref = k_ref if n % 2 == 0 else v_ref
        pairs.append((q_ref.at[:, columns(n)], o_ref.at[n, pl.ds(IN_Q, 128)]))
        pairs.append((g_ref.at[:, columns(n)], o_ref.at[n, pl.ds(IN_G, 128)]))
        pairs.append((x_ref.at[:, columns(n // 4)], o_ref.at[n, pl.ds(IN_X, 128)]))
    copies = begin(pairs, sems)
    for n in range(HEADS):
        o_ref[n, IN_S : IN_S + 16] = s_ref[...]
    finish(copies)


def block_of(i, st_ref):
    start = st_ref[i]
    lane = lax.broadcasted_iota(jnp.int32, (1, TQ), 1)
    part = lane // HALF
    upper = i >= QB // 2
    source = (i - QB // 2) * QS + part
    block = jnp.where(upper, 2 * MEMBERS - 1 - source, i * QS + part)
    last = BACK + block * HALF + lane % HALF
    return start, last, jnp.min(start) // TK, jnp.max(last) // TK + 1


def masked(s, start, last, base, turned, fill=NEG):
    rows = lax.broadcasted_iota(jnp.int32, (HALF, TQ), 0)
    parts = []
    for b in range(KS):
        off = base + HALF * jnp.where(turned, KS - 1 - b, b)
        seen = (rows >= start - off) & (rows <= last - off)
        parts.append(jnp.where(seen, s[b * HALF : (b + 1) * HALF], fill))
    return jnp.concatenate(parts, axis=0)


def own_tile(t):
    u = t - BACK_TILES
    turned = u >= OWN_TILES // 2
    return jnp.where(turned, OWN_TILES + OWN_TILES // 2 - 1 - u, u), turned


def back_tile(t):
    return BACK_TILES - 1 - t, True


def rows_of(ref, at, count):
    return ref[pl.ds(at * count, count)].reshape(count * HALF, HEAD)


def softmax_tiles(lo, hi, place, qi, start, last, k_at, vt_s, carry):
    def tile(t, carry):
        m, l8, acc = carry
        at, turned = place(t)
        s = dot(k_at(at), qi, NT) * FOLD
        s = masked(s, start, last, t * TK, turned)
        m_new = jnp.maximum(m, jnp.max(s, axis=0, keepdims=True))
        p = jnp.exp2(s - m_new)
        keep = jnp.exp2(m - m_new)
        l8 = l8 * keep + jnp.sum(p.reshape(TK // 8, 8, TQ), axis=0)
        acc = acc * keep + dot(vt_s[at], p.astype(BF))
        return m_new, l8, acc

    return lax.fori_loop(lo, hi, tile, carry)


def grad_tiles(lo, hi, place, qi, gi, start, last, lse, delta, k_at, v_at, kt_s, dk_s, dv_s, dq):
    def tile(t, dq):
        at, turned = place(t)
        s = masked(dot(k_at(at), qi, NT) * FOLD - lse, start, last, t * TK, turned)
        p = jnp.exp2(s)
        dp = dot(v_at(at), gi, NT)
        ds = (p * (dp - delta)).astype(BF)
        dv_s[at] += dot(p.astype(BF), gi)
        dk_s[at] += dot(ds, qi)
        return dq + dot(kt_s[at], ds)

    return lax.fori_loop(lo, hi, tile, dq)


def forward_own_kernel(core_ref, a_ref, x_ref, st_ref, m_ref, l_ref, acc_ref, q_s, kv_s, s_s, vt_s, acc_s, sems):
    core = core_ref[0]
    copies = begin(
        halves(a_ref, IN_X, kv_s.at[core])
        + halves(x_ref, 0, kv_s.at[1 - core])
        + [(a_ref.at[:, pl.ds(IN_S, 16)], s_s)]
        + halves(a_ref, IN_Q, q_s),
        sems,
    )
    finish(copies[:5])
    for t in range(SPAN // 128):
        s0, row = (2 * t, 0) if t < 8 else (2 * t - 16, 2)
        both = s_s[s0].astype(F32) + s_s[s0 + 1].astype(F32)
        start = both[row : row + 1] * 64.0 + both[row + 1 : row + 2]
        c = (t % 4) * 128
        st_ref[t // 4, 0:1, c : c + 128] = start.astype(jnp.int32)
    for t in range(OWN_TILES):
        vt_s[t] = rows_of(kv_s.at[1], t, KS).T
    finish(copies[5:])

    def q_block(i, _):
        qi = rows_of(q_s, i, QS)
        start, last, first, end = block_of(i, st_ref)
        m, l8, acc = softmax_tiles(
            jnp.maximum(first, BACK_TILES),
            end,
            own_tile,
            qi,
            start,
            last,
            lambda at: rows_of(kv_s.at[0], at, KS),
            vt_s,
            (jnp.full((1, TQ), NEG, F32), jnp.zeros((8, TQ), F32), jnp.zeros((HEAD, TQ), F32)),
        )
        m_ref[i] = m
        l_ref[i] = jnp.sum(l8, axis=0, keepdims=True)
        acc_s[i] = acc
        pltpu.make_async_copy(acc_s.at[i], acc_ref.at[i], sems.at[7 + i]).start()
        return 0

    lax.fori_loop(0, QB, q_block, 0)
    for i in range(QB):
        pltpu.make_async_copy(acc_s.at[i], acc_ref.at[i], sems.at[7 + i]).wait()


def back_kernel(
    core_ref, a_ref, p_ref, x_ref, st_ref, m_ref, l_ref, acc_ref,
    lse_ref, delta_ref, out_ref, dq_ref, keep_ref, give_ref,
    q_s, g_s, kv_s, vt_s, kt_s, acc_s, dq_s, o_s, dk_s, dv_s, sems,
):
    core = core_ref[0]
    copies = begin(
        [(p_ref, kv_s.at[core]), (x_ref, kv_s.at[1 - core])]
        + halves(a_ref, IN_Q, q_s)
        + halves(a_ref, IN_G, g_s)
        + [(acc_ref, acc_s)],
        sems,
    )
    finish(copies[:2])
    for t in range(BACK_TILES):
        kt_s[t] = rows_of(kv_s.at[0], t, KS).T
        vt_s[t] = rows_of(kv_s.at[1], t, KS).T
    dk_s[...] = jnp.zeros_like(dk_s)
    dv_s[...] = jnp.zeros_like(dv_s)
    finish(copies[2:])

    def outs(i):
        at, row = i // 2, i % 2
        return pltpu.make_async_copy(
            o_s.at[pl.ds(i * QS, QS)],
            out_ref.at[pl.ds((i % 2) * QS, QS), pl.ds(pl.multiple_of(OUT_A + (i // 2) * HALF, HALF), HALF)],
            sems.at[7 + i],
        )

    def dqs(i):
        return pltpu.make_async_copy(dq_s.at[i], dq_ref.at[i], sems.at[11 + i])

    def q_block(i, _):
        qi = rows_of(q_s, i, QS)
        gi = rows_of(g_s, i, QS)
        start, last, first, end = block_of(i, st_ref)
        l8 = jnp.concatenate([l_ref[i], jnp.zeros((7, TQ), F32)], axis=0)
        m, l8, acc = softmax_tiles(
            first,
            BACK_TILES,
            back_tile,
            qi,
            start,
            last,
            lambda at: rows_of(kv_s.at[0], at, KS),
            vt_s,
            (m_ref[i], l8, acc_s[i]),
        )
        l = jnp.sum(l8, axis=0, keepdims=True)
        out_t = acc * (1.0 / l)
        lse = m + jnp.log2(l)
        lse_ref[i] = lse
        delta = jnp.sum(out_t * gi.astype(F32).T, axis=0, keepdims=True)
        delta_ref[i] = delta
        o_s[pl.ds(i * QS, QS)] = out_t.T.astype(BF).reshape(QS, HALF, HEAD)
        outs(i).start()
        dq_s[i] = grad_tiles(
            first,
            BACK_TILES,
            back_tile,
            qi,
            gi,
            start,
            last,
            lse,
            delta,
            lambda at: rows_of(kv_s.at[0], at, KS),
            lambda at: rows_of(kv_s.at[1], at, KS),
            kt_s,
            dk_s,
            dv_s,
            jnp.zeros((HEAD, TQ), F32),
        )
        dqs(i).start()
        return 0

    lax.fori_loop(0, QB, q_block, 0)
    even = core == 0
    for t in range(BACK_TILES):
        dk, dv = dk_s[t] * SCALE, dv_s[t]
        at = slice(t * KS, (t + 1) * KS)
        keep_ref[at] = jnp.where(even, dk, dv).astype(BF).reshape(KS, HALF, HEAD)
        give_ref[at] = jnp.where(even, dv, dk).astype(BF).reshape(KS, HALF, HEAD)
    for i in range(QB):
        outs(i).wait()
        dqs(i).wait()


def own_kernel(
    core_ref, a_ref, x_ref, st_ref, lse_ref, delta_ref, dq_ref, old_ref, after_ref,
    out_ref, keep_ref, give_ref,
    q_s, g_s, kv_s, kt_s, dq_s, o_s, dk_s, dv_s, sems,
):
    core = core_ref[0]
    copies = begin(
        halves(a_ref, IN_X, kv_s.at[core])
        + halves(x_ref, 0, kv_s.at[1 - core])
        + halves(a_ref, IN_Q, q_s)
        + halves(a_ref, IN_G, g_s)
        + [(dq_ref, dq_s)],
        sems,
    )
    dk_s[...] = jnp.zeros_like(dk_s)
    dv_s[...] = jnp.zeros_like(dv_s)
    finish(copies[:4])
    for t in range(OWN_TILES):
        kt_s[t] = rows_of(kv_s.at[0], t, KS).T
    finish(copies[4:])

    def outs(i):
        return pltpu.make_async_copy(
            o_s.at[pl.ds(i * QS, QS)],
            out_ref.at[pl.ds((i % 2) * QS, QS), pl.ds(pl.multiple_of(OUT_Q + (i // 2) * HALF, HALF), HALF)],
            sems.at[9 + i],
        )

    def q_block(i, _):
        qi = rows_of(q_s, i, QS)
        gi = rows_of(g_s, i, QS)
        start, last, first, end = block_of(i, st_ref)
        dq = grad_tiles(
            jnp.maximum(first, BACK_TILES),
            end,
            own_tile,
            qi,
            gi,
            start,
            last,
            lse_ref[i],
            delta_ref[i],
            lambda at: rows_of(kv_s.at[0], at, KS),
            lambda at: rows_of(kv_s.at[1], at, KS),
            kt_s,
            dk_s,
            dv_s,
            dq_s[i],
        )
        o_s[pl.ds(i * QS, QS)] = (dq * SCALE).T.astype(BF).reshape(QS, HALF, HEAD)
        outs(i).start()
        return 0

    lax.fori_loop(0, QB, q_block, 0)
    even = core == 0
    for t in range(OWN_TILES):
        dk, dv = dk_s[t] * SCALE, dv_s[t]
        half, s0 = t // (OWN_TILES // 2), (t % (OWN_TILES // 2)) * KS
        at = (slice(s0, s0 + KS), slice(half * HALF, half * HALF + HALF))
        keep_ref[at] = jnp.where(even, dk, dv).astype(BF).reshape(KS, HALF, HEAD)
        give_ref[at] = jnp.where(even, dv, dk).astype(BF).reshape(KS, HALF, HEAD)
    for i in range(QB):
        outs(i).wait()


def tie_kernel(x_ref, after_ref, o_ref, sems):
    del x_ref, after_ref, o_ref, sems


def merge_kernel(keep_ref, got_ref, back_ref, old_ref, out_ref, x_s, sems):
    lower, upper = slice(0, HALF), slice(HALF, 2 * HALF)
    x_s[:, lower] = (keep_ref[:, lower].astype(F32) + got_ref[:, lower].astype(F32)).astype(BF)
    total = keep_ref[:, upper].astype(F32) + got_ref[:, upper].astype(F32)
    x_s[:, upper] = (total + back_ref[...].astype(F32)).astype(BF)
    finish(begin([(x_s, out_ref.at[:, pl.ds(OUT_X, 128)])], sems))


def unpack_kernel(t_ref, a_ref, q_ref, k_ref, v_ref, sems):
    pairs = []
    for n in range(HEADS):
        pairs.append((t_ref.at[n, pl.ds(OUT_A, 128)], a_ref.at[:, columns(n)]))
        pairs.append((t_ref.at[n, pl.ds(OUT_Q, 128)], q_ref.at[:, columns(n)]))
    copies = begin(pairs, sems)
    for g in range(GROUPS):
        at = slice(g * HEAD, (g + 1) * HEAD)
        for n, o_ref in ((4 * g, k_ref), (4 * g + 1, v_ref)):
            total = t_ref[n, OUT_X : OUT_X + 128].astype(F32) + t_ref[
                n + 2, OUT_X : OUT_X + 128
            ].astype(F32)
            o_ref[:, at] = total.astype(BF)
    finish(copies)


def shape(dims, dtype=BF):
    return jax.ShapeDtypeStruct(dims, dtype)


HBM = pl.BlockSpec(memory_space=pltpu.HBM)
VMEM = pl.BlockSpec(memory_space=pltpu.VMEM)
SMEM = pl.BlockSpec(memory_space=pltpu.SMEM)


def call(kernel, name, us, ins, outs, scratch, copies, mib=32, **more):
    return pl.pallas_call(
        kernel,
        in_specs=ins,
        out_specs=[space for space, _ in outs],
        out_shape=[what for _, what in outs],
        scratch_shapes=scratch + [pltpu.SemaphoreType.DMA((copies,))],
        compiler_params=pltpu.CompilerParams(vmem_limit_bytes=mib * 1024 * 1024),
        cost_estimate=pl.CostEstimate(
            flops=int(us * 4e8), bytes_accessed=1 << 20, transcendentals=0
        ),
        name=name,
        **more,
    )


def tie(x, after):
    (x,) = call(
        tie_kernel,
        "tie",
        1,
        [HBM, HBM],
        [(HBM, shape(x.shape))],
        [],
        1,
        input_output_aliases={0: 0},
    )(x, after)
    return x


def on_device(queries, key_states, value_vectors, grad_out, doc_start):
    cycle = lax.axis_index("dp")
    core = lax.axis_index("ctx") % 2
    q = queries.reshape(128, HEADS * HEAD)
    g = grad_out.reshape(128, HEADS * HEAD)
    k = key_states.reshape(128, GROUPS * HEAD)
    v = value_vectors.reshape(128, GROUPS * HEAD)
    swap = [(i, i ^ 1) for i in range(MEMBERS)]
    which = core.reshape(1)

    rel = doc_start.reshape(2, HALF) - (cycle * SPAN - BACK)
    parts = jnp.stack([rel // 64, rel % 64], axis=1).reshape(4, HALF).astype(BF)
    zero = jnp.zeros_like(parts)
    starts = jnp.where(
        core == 0,
        jnp.concatenate([parts, zero], axis=1),
        jnp.concatenate([zero, parts], axis=1),
    )
    starts = jnp.pad(starts, ((0, 12), (0, 0)))

    rows = pltpu.VMEM((2 * MEMBERS, HALF, HEAD), BF)
    own_kv = pltpu.VMEM((2, 2 * MEMBERS, HALF, HEAD), BF)
    back_kv = pltpu.VMEM((2, MEMBERS, HALF, HEAD), BF)
    wide = pltpu.VMEM((QB, HEAD, TQ), F32)
    line = (VMEM, shape((QB, 1, TQ), F32))

    def turned(tiles):
        return pltpu.VMEM((tiles, HEAD, TK), BF)

    def sums(tiles):
        return pltpu.VMEM((tiles, TK, HEAD), F32)

    (a,) = call(
        pack_kernel,
        "pack",
        1,
        [HBM, HBM, HBM, HBM, VMEM],
        [(VMEM, shape((HEADS, IN_ROWS, HEAD)))],
        [],
        3 * HEADS,
    )(*(pltpu.with_memory_space_constraint(each, pltpu.HBM) for each in (q, g, k, v)), starts)
    a = lax.all_to_all(a, "ctx", 0, 0, tiled=True)
    x = lax.ppermute(a[:, IN_X : IN_X + 128], "ctx", swap)
    p = lax.ppermute(a[:, IN_X + HALF : IN_X + 128], "dp", [(i, i + 1) for i in range(15)])
    st, m, l, acc = call(
        forward_own_kernel,
        "forward_own",
        9,
        [SMEM, HBM, HBM],
        [(VMEM, shape((QB, 1, TQ), jnp.int32)), line, line, (HBM, shape((QB, HEAD, TQ), F32))],
        [rows, own_kv, pltpu.VMEM((MEMBERS, 16, HEAD), BF), turned(OWN_TILES), wide],
        7 + QB,
    )(which, a, x)
    p = tie(p, m)
    px = lax.ppermute(p, "ctx", swap)
    lse, delta, out, dq, keep_back, give_back = call(
        back_kernel,
        "back",
        7,
        [SMEM, HBM, HBM, HBM, VMEM, VMEM, VMEM, HBM],
        [
            line,
            line,
            (HBM, shape((MEMBERS, OUT_ROWS, HEAD))),
            (HBM, shape((QB, HEAD, TQ), F32)),
            (VMEM, shape((MEMBERS, HALF, HEAD))),
            (VMEM, shape((MEMBERS, HALF, HEAD))),
        ],
        [rows, rows, back_kv, turned(BACK_TILES), turned(BACK_TILES), wide, wide, rows]
        + [sums(BACK_TILES), sums(BACK_TILES)],
        7 + 2 * QB,
    )(which, a, p, px, st, m, l, acc)
    got_back = lax.ppermute(give_back, "ctx", swap)
    back = (keep_back.astype(F32) + got_back.astype(F32)).astype(BF)
    sent_back = lax.ppermute(back, "dp", [(i + 1, i) for i in range(15)])
    out, keep, give = call(
        own_kernel,
        "own",
        11,
        [SMEM, HBM, HBM, VMEM, VMEM, VMEM, HBM, HBM, HBM],
        [
            (HBM, shape((MEMBERS, OUT_ROWS, HEAD))),
            (VMEM, shape((MEMBERS, 128, HEAD))),
            (VMEM, shape((MEMBERS, 128, HEAD))),
        ],
        [rows, rows, own_kv, turned(OWN_TILES), wide, rows, sums(OWN_TILES), sums(OWN_TILES)],
        9 + QB,
        input_output_aliases={7: 0},
    )(which, a, x, st, lse, delta, dq, out, back)
    got = lax.ppermute(tie(give, sent_back), "ctx", swap)
    (out,) = call(
        merge_kernel,
        "merge",
        1,
        [VMEM, VMEM, VMEM, HBM],
        [(HBM, shape((MEMBERS, OUT_ROWS, HEAD)))],
        [pltpu.VMEM((MEMBERS, 128, HEAD), BF)],
        1,
        input_output_aliases={3: 0},
    )(keep, got, sent_back, out)
    out = lax.all_to_all(out, "ctx", 0, 0, tiled=True)
    attn, q_grad, k_grad, v_grad = call(
        unpack_kernel,
        "unpack",
        2,
        [VMEM],
        [(HBM, shape(q.shape)), (HBM, shape(q.shape)), (VMEM, shape(k.shape)), (VMEM, shape(k.shape))],
        [],
        2 * HEADS,
    )(out)
    return (
        attn.reshape(queries.shape),
        q_grad.reshape(queries.shape),
        k_grad.reshape(key_states.shape),
        v_grad.reshape(value_vectors.shape),
    )


def solution(mesh):
    wide = P("dp", None, "ctx", None, None)
    return jax.shard_map(
        on_device,
        mesh=mesh,
        in_specs=(wide, wide, wide, wide, P("dp", None, "ctx", None)),
        out_specs=(wide, wide, wide, wide),
        check_vma=False,
    )
```

time: 132 us -> 113 us (0.86); the launches traced: 130 us -> 113 us
  blocking collectives: 74.4 us -> 53.3 us
  local copies, waits for them, and re-layouts: 4.89 us -> 0.08 us
  waiting for transfers between devices: 19 us -> 23.8 us
  Pallas kernels: 22.3 us -> 26.4 us
    all_to_all x2, blocking collectives: 74.4 us -> 53.3 us  [the longest x1 28.6 us: on_device(): a = lax.all_to_all(a, 'ctx', 0, 0, tiled=True)]
    ppermute x2 -> x6, waiting for transfers between devices: 19 us -> 23.8 us  [the longest x1 15.8 us: on_device(): sent_back = lax.ppermute(back, 'dp', [(i + 1, i) for i in range(15)])]
    pallas_call x4 -> x8, Pallas kernels: 22.3 us -> 26.4 us  [the longest x1 8.85 us: on_device(): call(own_kernel, 'own', 11, [SMEM, HBM, HBM, VMEM, VMEM, VMEM, HBM, HBM,...]
    unnamed x8 -> x0, local copies, waits for them, and re-layouts: 3.89 us -> none
    ppermute x2 -> x6, starting transfers between devices: 8.23 us -> 7.92 us  [the longest x1 5.41 us: on_device(): lax.ppermute(a[:, IN_X + HALF:IN_X + 128], 'dp', [(i, i + 1) for i in ran...]
  transfers between devices with their start and end apart: 2 -> 6, of which waited for: 2 -> 5; matrix products, arithmetic and copies ran while one was open for 1% -> 0% of each run, Pallas kernels for 0% -> 15%
where the time goes in v2:
time: 113 us
  blocking collectives  53.3 us (47%)
  Pallas kernels  26.4 us (23%)
  waiting for transfers between devices  23.8 us (21%)
  starting transfers between devices  7.92 us (7%)
    all_to_all x1, blocking collectives, on_device(): a = lax.all_to_all(a, 'ctx', 0, 0, tiled=True)  28.6 us
    all_to_all x1, blocking collectives, on_device(): out = lax.all_to_all(out, 'ctx', 0, 0, tiled=True)  24.7 us
    ppermute x1, waiting for transfers between devices, on_device(): sent_back = lax.ppermute(back, 'dp', [(i + 1, i) for i in range(15)])  15.8 us
    pallas_call x1, Pallas kernels, on_device(): call(own_kernel, 'own', 11, [SMEM, HBM, HBM, VMEM, VMEM, VMEM, HBM, HBM,...  8.85 us
    pallas_call x1, Pallas kernels, on_device(): call(forward_own_kernel, 'forward_own', 9, [SMEM, HBM, HBM], [(VMEM, shap...  7.75 us
    pallas_call x1, Pallas kernels, on_device(): call(back_kernel, 'back', 7, [SMEM, HBM, HBM, HBM, VMEM, VMEM, VMEM, HBM]...  5.87 us
    ppermute x1, starting transfers between devices, on_device(): lax.ppermute(a[:, IN_X + HALF:IN_X + 128], 'dp', [(i, i + 1) for i in ran...  5.41 us
    ppermute x1, waiting for transfers between devices, on_device(): lax.ppermute(a[:, IN_X + HALF:IN_X + 128], 'dp', [(i, i + 1) for i in ran...  3.12 us
  transfers between devices with their start and end apart: 6, of which 5 were waited for; matrix products, arithmetic and copies ran while one was open for 0% of the time, Pallas kernels for 15%

profile of v2, /device:TPU:70, one launch (start us, length us, event | category | flops | bytes accessed | tf_op | source)
XLA Modules:
  0.0 113.1 jit_solution(14095247172445920451)
XLA Ops:
  0.6 0.7 broadcast_subtract_fusion
  1.4 0.1 pad_select_fusion
  1.5 1.8 %pack.1 = bf16[16,400,128]{2,1,0:T(8,128)(2,1)S(1)} custom-call(bf16[128,2048]{1,0:T(8,128)(2,1)} %bitcast.19, bf16[128,2048]{1,0:T(8,128)(2,1)} %bitcast.20, bf16[128,512]{1,0:T(8,128)(2,1)} %bitcast.21, bf16[128,512]{1,0:T(8,128)(2,1)} %bitcast.22, bf16[16,128]{1,0:T(8,128)(2,1)S(1)} %pad.6.s_ref), custom_call_target="tpu_custom_call" | custom-call | flops 400000000 | bytes 1048576 | tf_op jit(solution)/shard_map/pack/pallas_call | solution.py:437
  3.3 28.6 %all_to_all.10.a_ref = bf16[16,400,128]{2,1,0:T(8,128)(2,1)S(1)} all-to-all(bf16[16,400,128]{2,1,0:T(8,128)(2,1)S(1)} %pack.1), channel_id=1, replica_groups=mesh['dp'=16,'ctx'=16] {'ctx'}, dimensions={0} | all-to-all | bytes 3276800 | tf_op jit(solution)/shard_map/all_to_all | solution.py:446
  31.9 0.2 collective-permute-start
  32.0 5.4 %collective-permute-start.1 = (bf16[16,64,128]{2,1,0:T(8,128)(2,1)S(1)}, bf16[16,64,128]{2,1,0:T(8,128)(2,1)S(1)}, u32[]{:S(2)}, u32[]{:S(2)}) collective-permute-start(bf16[16,64,128]{2,1,0:T(8,128)(2,1)S(1)} %slice.9), channel_id=1, source_target_pairs={{0,16},{16,32},{32,48},{48,64},{64,80},{80,96},{96,112},{112,128},... | collective-permute-start | bytes 786440 | tf_op jit(solution)/shard_map/ppermute | solution.py:448
  37.5 0.0 collective-permute-done.x_ref
  37.5 7.8 %forward_own.1 = (s32[4,1,512]{2,1,0:T(1,128)S(1)}, f32[4,1,512]{2,1,0:T(1,128)S(1)}, f32[4,1,512]{2,1,0:T(1,128)S(1)}, f32[4,128,512]{2,1,0:T(8,128)S(1)}) custom-call(s32[1]{0:T(128)} %bitcast.core_ref, bf16[16,400,128]{2,1,0:T(8,128)(2,1)S(1)} %all_to_all.10.a_ref, bf16[16,128,128]{2,1,0:T(8,128)(2,1)S(1)} %collective-permute-done.x_ref), custom_call_target="tpu_custom_call" | custom-call | flops 3600000000 | bytes 1048576 | tf_op jit(solution)/shard_map/forward_own/pallas_call | solution.py:449
  45.2 3.1 %collective-permute-done.1.x_ref = bf16[16,64,128]{2,1,0:T(8,128)(2,1)S(1)} collective-permute-done((bf16[16,64,128]{2,1,0:T(8,128)(2,1)S(1)}, bf16[16,64,128]{2,1,0:T(8,128)(2,1)S(1)}, u32[]{:S(2)}, u32[]{:S(2)}) %collective-permute-start.1) | collective-permute-done | bytes 262176 | tf_op jit(solution)/shard_map/ppermute | solution.py:448
  48.4 0.1 collective-permute-start.2
  48.5 1.5 %collective-permute-done.2.x_ref = bf16[16,64,128]{2,1,0:T(8,128)(2,1)S(1)} collective-permute-done((bf16[16,64,128]{2,1,0:T(8,128)(2,1)S(1)}, bf16[16,64,128]{2,1,0:T(8,128)(2,1)S(1)}, u32[]{:S(2)}, u32[]{:S(2)}) %collective-permute-start.2) | collective-permute-done | bytes 262176 | tf_op jit(solution)/shard_map/ppermute | solution.py:459
  50.0 5.9 %back.1 = (f32[4,1,512]{2,1,0:T(1,128)S(1)}, f32[4,1,512]{2,1,0:T(1,128)S(1)}, bf16[16,384,128]{2,1,0:T(8,128)(2,1)S(1)}, f32[4,128,512]{2,1,0:T(8,128)S(1)}, bf...) custom-call(s32[1]{0:T(128)} %bitcast.core_ref, bf16[16,400,128]{2,1,0:T(8,128)(2,1)S(1)} %all_to_all.10.a_ref, ...), custom_call_target="tpu_custom_call" | custom-call | flops 2800000000 | bytes 1048576 | tf_op jit(solution)/shard_map/back/pallas_call | solution.py:460
  55.9 0.2 collective-permute-start.3
  56.1 1.4 %collective-permute-done.3 = bf16[16,64,128]{2,1,0:T(8,128)(2,1)S(1)} collective-permute-done((bf16[16,64,128]{2,1,0:T(8,128)(2,1)S(1)}, bf16[16,64,128]{2,1,0:T(8,128)(2,1)S(1)}, u32[]{:S(2)}, u32[]{:S(2)}) %collective-permute-start.3) | collective-permute-done | bytes 262176 | tf_op jit(solution)/shard_map/ppermute | solution.py:477
  57.5 0.1 add_convert_fusion.after_ref
  57.6 1.9 %collective-permute-start.4 = (bf16[16,64,128]{2,1,0:T(8,128)(2,1)S(1)}, bf16[16,64,128]{2,1,0:T(8,128)(2,1)S(1)}, u32[]{:S(2)}, u32[]{:S(2)}) collective-permute-start(bf16[16,64,128]{2,1,0:T(8,128)(2,1)S(1)} %add_convert_fusion.after_ref), channel_id=1, source_target_pairs={{16,0},{32,16},{48,32},{64,48},{80,64},{96,80},{112,96},{128,112},... | collective-permute-start | bytes 786440 | tf_op jit(solution)/shard_map/ppermute | solution.py:479
  59.5 8.9 %own.1 = (bf16[16,384,128]{2,1,0:T(8,128)(2,1)S(1)}, bf16[16,128,128]{2,1,0:T(8,128)(2,1)S(1)}, bf16[16,128,128]{2,1,0:T(8,128)(2,1)S(1)}) custom-call(s32[1]{0:T(128)} %bitcast.core_ref, bf16[16,400,128]{2,1,0:T(8,128)(2,1)S(1)} %all_to_all.10.a_ref, bf16[16,128,128]{2,1,0:T(8,128)(2,1)S(1)} %collective-permute-done.x_ref, ...), custom_call_target="tpu_custom_call", output_to_operand_aliasing={{0}: (7, {})} | custom-call | flops 4400000000 | bytes 1048576 | tf_op jit(solution)/shard_map/own/pallas_call | solution.py:480
  68.3 15.8 %collective-permute-done.4.after_ref.back_ref = bf16[16,64,128]{2,1,0:T(8,128)(2,1)S(1)} collective-permute-done((bf16[16,64,128]{2,1,0:T(8,128)(2,1)S(1)}, bf16[16,64,128]{2,1,0:T(8,128)(2,1)S(1)}, u32[]{:S(2)}, u32[]{:S(2)}) %collective-permute-start.4) | collective-permute-done | bytes 262176 | tf_op jit(solution)/shard_map/ppermute | solution.py:479
  84.2 0.1 collective-permute-start.5
  84.3 1.9 %collective-permute-done.5.got_ref = bf16[16,128,128]{2,1,0:T(8,128)(2,1)S(1)} collective-permute-done((bf16[16,128,128]{2,1,0:T(8,128)(2,1)S(1)}, bf16[16,128,128]{2,1,0:T(8,128)(2,1)S(1)}, u32[]{:S(2)}, u32[]{:S(2)}) %collective-permute-start.5) | collective-permute-done | bytes 524320 | tf_op jit(solution)/shard_map/ppermute | solution.py:494
  86.2 0.2 merge.1
  86.4 24.7 %all_to_all.11.t_ref = bf16[16,384,128]{2,1,0:T(8,128)(2,1)S(1)} all-to-all(bf16[16,384,128]{2,1,0:T(8,128)(2,1)S(1)} %merge.1), channel_id=1, replica_groups=mesh['dp'=16,'ctx'=16] {'ctx'}, dimensions={0} | all-to-all | bytes 3145728 | tf_op jit(solution)/shard_map/all_to_all | solution.py:505
  111.1 1.9 %unpack.1 = (bf16[128,2048]{1,0:T(8,128)(2,1)}, bf16[128,2048]{1,0:T(8,128)(2,1)}, bf16[128,512]{1,0:T(8,128)(2,1)}, bf16[128,512]{1,0:T(8,128)(2,1)}) custom-call(bf16[16,384,128]{2,1,0:T(8,128)(2,1)S(1)} %all_to_all.11.t_ref), custom_call_target="tpu_custom_call" | custom-call | flops 800000000 | bytes 1048576 | tf_op jit(solution)/shard_map/unpack/pallas_call | solution.py:506
  (8 shorter events, 0.1 us)
Async XLA Ops:
  31.9 5.6 %collective-permute-start = (bf16[16,128,128]{2,1,0:T(8,128)(2,1)S(1)}, bf16[16,128,128]{2,1,0:T(8,128)(2,1)S(1)}, u32[]{:S(2)}, u32[]{:S(2)}) collective-permute-start(bf16[16,128,128]{2,1,0:T(8,128)(2,1)S(1)} %slice.8), channel_id=1, source_target_pairs={{0,1},{1,0},{2,3},{3,2},{4,5},{5,4},{6,7},{7,6},{8,9},{9,8},{10,11... | collective-permute-start | bytes 1572872 | tf_op jit(solution)/shard_map/ppermute | solution.py:447
  32.0 16.3 %collective-permute-start.1 = (bf16[16,64,128]{2,1,0:T(8,128)(2,1)S(1)}, bf16[16,64,128]{2,1,0:T(8,128)(2,1)S(1)}, u32[]{:S(2)}, u32[]{:S(2)}) collective-permute-start(bf16[16,64,128]{2,1,0:T(8,128)(2,1)S(1)} %slice.9), channel_id=1, source_target_pairs={{0,16},{16,32},{32,48},{48,64},{64,80},{80,96},{96,112},{112,128},... | collective-permute-start | bytes 786440 | tf_op jit(solution)/shard_map/ppermute | solution.py:448
  48.4 1.6 %collective-permute-start.2 = (bf16[16,64,128]{2,1,0:T(8,128)(2,1)S(1)}, bf16[16,64,128]{2,1,0:T(8,128)(2,1)S(1)}, u32[]{:S(2)}, u32[]{:S(2)}) collective-permute-start(bf16[16,64,128]{2,1,0:T(8,128)(2,1)S(1)} %tie.2.p_ref), channel_id=1, source_target_pairs={{0,1},{1,0},{2,3},{3,2},{4,5},{5,4},{6,7},{7,6},{8,9},{9,8},{10,11... | collective-permute-start | bytes 786440 | tf_op jit(solution)/shard_map/ppermute | solution.py:459
  55.9 1.6 %collective-permute-start.3 = (bf16[16,64,128]{2,1,0:T(8,128)(2,1)S(1)}, bf16[16,64,128]{2,1,0:T(8,128)(2,1)S(1)}, u32[]{:S(2)}, u32[]{:S(2)}) collective-permute-start(bf16[16,64,128]{2,1,0:T(8,128)(2,1)S(1)} %get-tuple-element.30), channel_id=1, source_target_pairs={{0,1},{1,0},{2,3},{3,2},{4,5},{5,4},{6,7},{7,6},{8,9},{9,8},{10,11... | collective-permute-start | bytes 786440 | tf_op jit(solution)/shard_map/ppermute | solution.py:477
  57.6 26.6 %collective-permute-start.4 = (bf16[16,64,128]{2,1,0:T(8,128)(2,1)S(1)}, bf16[16,64,128]{2,1,0:T(8,128)(2,1)S(1)}, u32[]{:S(2)}, u32[]{:S(2)}) collective-permute-start(bf16[16,64,128]{2,1,0:T(8,128)(2,1)S(1)} %add_convert_fusion.after_ref), channel_id=1, source_target_pairs={{16,0},{32,16},{48,32},{64,48},{80,64},{96,80},{112,96},{128,112},... | collective-permute-start | bytes 786440 | tf_op jit(solution)/shard_map/ppermute | solution.py:479
  84.2 2.0 %collective-permute-start.5 = (bf16[16,128,128]{2,1,0:T(8,128)(2,1)S(1)}, bf16[16,128,128]{2,1,0:T(8,128)(2,1)S(1)}, u32[]{:S(2)}, u32[]{:S(2)}) collective-permute-start(bf16[16,128,128]{2,1,0:T(8,128)(2,1)S(1)} %tie.3), channel_id=1, source_target_pairs={{0,1},{1,0},{2,3},{3,2},{4,5},{5,4},{6,7},{7,6},{8,9},{9,8},{10,11... | collective-permute-start | bytes 1572872 | tf_op jit(solution)/shard_map/ppermute | solution.py:494
